TPU v7x, 32 devices: a whole 2x2x4 slice. The times are simulated.
32 devices in a mesh: dp: 4 (over y, x), row: 2 (over core), col: 4 (over z).
Axes of the slice: x: 2, y: 2, z: 4, core: 2. Of those that a mesh axis runs over, the one named last changes fastest.
Arguments:
- hidden: bfloat16 [4096, 14336], P('dp', 'row'), may hold values from -6 to 6
- upstream: bfloat16 [4096, 4096], P('dp', 'col'), may hold values from -0.09375 to 0.09375
- first_codes: int32 [14336, 4096], P(('row', 'dp'), 'col'), may hold values from 0 to 15
- first_scale: float32 [14336, 32], P(('row', 'dp'), 'col'), may hold values from 0.1 to 1
- second_codes: int32 [14336, 4096], P(('row', 'dp'), 'col'), may hold values from 0 to 15
- second_rows: float32 [14336], P(('row', 'dp')), may hold values from 0.004 to 0.04
- second_columns: float32 [4096], P('col'), may hold values from 0.004 to 0.04
Outputs:
- update_step: float32 [14336, 4096], P(('row', 'dp'), 'col')
- first_normed: bfloat16 [14336, 4096], P(('row', 'dp'), 'col')
- first_peak: float32 [14336, 32], P(('row', 'dp'), 'col')
- second_normed: bfloat16 [14336, 4096], P(('row', 'dp'), 'col')
- row_peak: float32 [14336], P(('row', 'dp'))
- column_peak: float32 [4096], P('col')
All inputs are finite; a program needn't handle non-finite values. Where the computation divides by a largest or mean magnitude, that divisor is 1e-20 or more.
Results may differ from a plain program's by a relative error of at most 0.015.
Values may be sent and summed in bfloat16 or wider, within the bound.
A program may use at most 128 MiB of HBM per device.

v0:
```python
import jax
import jax.numpy as jnp
from jax import lax
from jax.sharding import PartitionSpec as P

STEP = 10


def first_table(codes):
    level = codes.astype(jnp.float32)
    upper = level >= 8.0
    expo = jnp.where(upper, level - 8.0, 7.0 - level)
    magnitude = jnp.where(expo > 0.0, jnp.exp2(expo - 7.0), 0.0 * expo)
    return jnp.where(upper, magnitude, -magnitude)


def contract_tokens(left, right):
    return lax.dot_general(
        left, right, (((0,), (0,)), ((), ())), preferred_element_type=jnp.float32
    )


def per_device(
    hidden, upstream, first_codes, first_scale, second_codes, second_rows, second_columns
):
    rows_own = first_codes.shape[0]
    columns = first_codes.shape[1]
    block_count = first_scale.shape[1]
    gradient = lax.psum_scatter(
        contract_tokens(hidden, upstream).astype(jnp.bfloat16),
        "dp",
        scatter_dimension=0,
        tiled=True,
    ).astype(jnp.float32)
    shaped = gradient.reshape(rows_own, block_count, -1)
    first_old = first_scale[:, :, None] * first_table(first_codes).reshape(
        rows_own, block_count, -1
    )
    level_two = (second_codes.astype(jnp.float32) + 1.0) / 16.0
    second_old = (jnp.minimum(second_rows[:, None], second_columns[None, :]) * level_two).reshape(
        rows_own, block_count, -1
    )
    first_new = 0.9 * first_old + 0.1 * shaped
    second_new = 0.999 * second_old + 0.001 * shaped * shaped
    corr_one = 1.0 - 0.9**STEP
    corr_two = 1.0 - 0.999**STEP
    update_step = first_new / corr_one / (jnp.sqrt(second_new / corr_two) + 1e-08)
    first_peak = jnp.max(jnp.abs(first_new), axis=2)
    first_normed = (first_new / (first_peak[:, :, None] + 1e-06)).astype(jnp.bfloat16)
    second_flat = second_new.reshape(rows_own, columns)
    row_part = jnp.max(second_flat, axis=1)
    column_part = jnp.max(second_flat, axis=0)
    row_peak = lax.pmax(row_part, "col")
    column_peak = lax.pmax(column_part, ("dp", "row"))
    second_normed = (
        second_flat / (jnp.minimum(row_peak[:, None], column_peak[None, :]) + 1e-06)
    ).astype(jnp.bfloat16)
    return (
        update_step.reshape(rows_own, columns),
        first_normed.reshape(rows_own, columns),
        first_peak,
        second_normed,
        row_peak,
        column_peak,
    )


def solution(mesh):
    placed = (
        P("dp", "row"),
        P("dp", "col"),
        P(("row", "dp"), "col"),
        P(("row", "dp"), "col"),
        P(("row", "dp"), "col"),
        P(("row", "dp")),
        P("col"),
    )
    return jax.shard_map(
        per_device,
        mesh=mesh,
        in_specs=placed,
        out_specs=(
            P(("row", "dp"), "col"),
            P(("row", "dp"), "col"),
            P(("row", "dp"), "col"),
            P(("row", "dp"), "col"),
            P(("row", "dp")),
            P("col"),
        ),
        check_vma=False,
    )
```

profile of v0, /device:TPU:0, one launch (start us, length us, event | category | flops | bytes accessed | tf_op | source)
XLA Modules:
  0.0 245.7 jit_solution(13834492390965749872)
XLA Ops:
  7.2 0.0 copy-start
  7.2 0.0 reduce-scatter.2.cloned.1.call-start
  7.2 1.5 copy-done
  8.8 23.9 %convolution_convert_fusion = bf16[7168,1024]{1,0:T(8,128)(2,1)} fusion(bf16[1024,7168]{1,0:T(8,128)(2,1)} %param.7, bf16[1024,1024]{1,0:T(8,128)(2,1)S(1)} %copy-done), kind=kOutput, calls=%fused_computation | convolution fusion | flops 15039725568 | bytes 31457280 | tf_op jit(solution)/shard_map/dot_general | solution.py:18
  32.7 0.0 copy-start.4
  32.7 0.0 reduce-scatter.2.cloned.1.call-update
  32.7 0.8 copy-done.4
  33.5 0.3 copy.15
  33.8 5.4 %fusion.7 = f32[224,8,8,128]{3,1,2,0:T(8,128)S(1)} fusion(s32[1792,1024]{1,0:T(8,128)} %param.9), kind=kLoop, calls=%fused_computation.21 | loop fusion | flops 22020096 | bytes 14680064
  39.2 0.0 copy-start.7
  39.2 0.0 copy-start.8
  39.2 5.4 %copy.18 = f32[224,8,8,128]{3,2,1,0:T(8,128)} copy(f32[224,8,8,128]{3,1,2,0:T(8,128)S(1)} %fusion.7) | data formatting | bytes 14680064
  44.7 128.8 %reduce-scatter.2.cloned.1.call-done = bf16[1792,1024]{1,0:T(8,128)(2,1)} async-done(((bf16[7168,1024]{1,0:T(8,128)(2,1)}), bf16[1792,1024]{1,0:T(8,128)(2,1)}) %reduce-scatter.2.cloned.1.call-update) | async-done | bytes 3670032 | tf_op jit(solution)/shard_map/reduce_scatter | solution.py:29
  173.5 0.0 copy-done.7
  173.5 0.0 copy-done.8
  173.5 8.1 %fusion.8 = (f32[1792]{0:T(1024)S(1)}, f32[1024]{0:T(1024)S(1)}, f32[1792,1024]{1,0:T(8,128)}, f32[224,8,8,128]{3,1,2,0:T(8,128)S(1)}) fusion(bf16[1792,1024]{1,0:T(8,128)(2,1)} %reduce-scatter.2.cloned.1.call-done, s32[1792,1024]{1,0:T(8,128)} %param.11, f32[1024]{0:T(1024)S(1)} %copy-done.8, f32[1792]{0:T(1024)S(1)} %copy-done.7), kind=kLoop, calls=%fused_computation.22 | loop fusion | flops 23852288 | bytes 25712640 | tf_op jit(solution)/shard_map/reduce_max | solution.py:51
  181.5 0.0 copy-start.2
  181.5 1.8 copy.19
  183.3 1.3 copy-done.2
  184.6 4.3 %bitcast_add_fusion = f32[1792,8,128]{2,1,0:T(8,128)S(1)} fusion(f32[224,8,8,128]{3,2,1,0:T(8,128)S(1)} %copy.19, f32[224,8,8,128]{3,2,1,0:T(8,128)S(1)} %copy-done.2, f32[1792,8]{1,0:T(8,128)S(1)} %copy.15), kind=kLoop, calls=%fused_computation.9 | loop fusion | flops 5505024 | bytes 22077440 | tf_op jit(solution)/shard_map/add | solution.py:43
  189.0 3.0 %abs_reduce_fusion = f32[1792,8]{1,0:T(8,128)S(1)} fusion(f32[1792,8,128]{2,1,0:T(8,128)S(1)} %bitcast_add_fusion), kind=kLoop, calls=%fused_computation.15 | loop fusion | flops 3655680 | bytes 7397376 | tf_op jit(solution)/shard_map/reduce_max | solution.py:48
  192.0 0.9 copy.16
  192.9 1.0 broadcast_add_fusion
  193.9 0.0 copy-start.3
  193.9 12.0 %pmax.14 = f32[1792]{0:T(1024)S(1)} all-reduce(f32[1792]{0:T(1024)S(1)} %get-tuple-element.12), channel_id=1, replica_groups=mesh['dp'=4,'row'=2,'col'=4] {'col'}, use_global_device_ids=true, to_apply=%region_3.4 | all-reduce | flops 1792 | bytes 14336 | tf_op jit(solution)/shard_map/pmax | solution.py:53
  205.9 0.0 copy-start.5
  205.9 11.8 %pmax.15 = f32[1024]{0:T(1024)S(1)} all-reduce(f32[1024]{0:T(1024)S(1)} %get-tuple-element.13), channel_id=1, replica_groups=mesh['dp'=4,'row'=2,'col'=4] {'dp','row'}, use_global_device_ids=true, to_apply=%region_5.6 | all-reduce | flops 1024 | bytes 8192 | tf_op jit(solution)/shard_map/pmax | solution.py:54
  217.7 0.0 copy-start.6
  217.7 0.0 slice-start
  217.7 2.0 mul.64
  219.8 0.0 slice-start.1
  219.8 0.0 copy-done.3
  219.8 2.0 div.43
  221.9 0.0 copy-done.5
  221.9 0.0 copy-done.6
  221.9 0.0 slice-done
  221.9 0.0 slice-done.1
  221.9 0.0 copy-start.1
  221.9 17.0 %fusion.3 = (bf16[1792,1024]{1,0:T(8,128)(2,1)}, f32[1792,1024]{1,0:T(8,128)}, bf16[1792,1024]{1,0:T(8,128)(2,1)}) fusion(f32[224,8,8,128]{3,2,1,0:T(8,128)S(1)} %bitcast.33, bf16[1792,1024]{1,0:T(8,128)(2,1)} %reduce-scatter.2.cloned.1.call-done, s32[1792,1024]{1,0:T(8,128)S(1)} %bitcast.31, f32[224,8,8,128]{3,2,1,0:T(8,128)S(1)} %bitcast.32, ...), kind=kLoop, calls=%fused_computation.8 | loop fusion | flops 49545216 | bytes 47721472 | tf_op jit(solution)/shard_map/convert_element_type | solution.py:49
  238.9 0.0 copy-done.1
  (1 shorter events, 0.0 us)
Async XLA Ops:
  7.2 1.6 copy-start
  7.2 166.3 %reduce-scatter.2.cloned.1.call-start = ((), (), s32[]{:S(2)}) async-start(), calls=%async_computation.1 | async-start | bytes 18350080 | tf_op jit(solution)/shard_map/reduce_scatter | solution.py:29
  32.7 0.8 copy-start.4
  39.2 134.3 %copy-start.7 = (f32[1792]{0:T(1024)S(1)}, f32[1792]{0:T(1024)}, u32[]{:S(2)}) copy-start(f32[1792]{0:T(1024)} %param.12) | copy-start | bytes 21508
  39.2 134.3 %copy-start.8 = (f32[1024]{0:T(1024)S(1)}, f32[1024]{0:T(1024)}, u32[]{:S(2)}) copy-start(f32[1024]{0:T(1024)} %param.13) | copy-start | bytes 12292
  181.5 3.1 %copy-start.2 = (f32[224,8,8,128]{3,2,1,0:T(8,128)S(1)}, f32[224,8,8,128]{3,2,1,0:T(8,128)}, u32[]{:S(2)}) copy-start(f32[224,8,8,128]{3,2,1,0:T(8,128)} %copy.18) | copy-start | bytes 22020100
  193.9 25.9 %copy-start.3 = (f32[1792,8]{1,0:T(8,128)S(1)}, f32[1792,8]{1,0:T(8,128)}, u32[]{:S(2)}) copy-start(f32[1792,8]{1,0:T(8,128)} %broadcast_add_fusion) | copy-start | bytes 172036
  205.9 16.0 %copy-start.5 = (f32[1792]{0:T(1024)}, f32[1792]{0:T(1024)S(1)}, u32[]{:S(2)}) copy-start(f32[1792]{0:T(1024)S(1)} %pmax.14) | copy-start | bytes 21508
  217.7 4.2 %copy-start.6 = (f32[1024]{0:T(1024)}, f32[1024]{0:T(1024)S(1)}, u32[]{:S(2)}) copy-start(f32[1024]{0:T(1024)S(1)} %pmax.15) | copy-start | bytes 12292
  217.7 4.2 %slice-start = ((s8[7340032]{0:T(1024)(128)(4,1)}), s8[4194304]{0:T(1024)(128)(4,1)S(1)}, s32[]{:S(2)}) async-start(s8[7340032]{0:T(1024)(128)(4,1)} %bitcast.30), calls=%async_computation.2 | async-start | bytes 8388608
  219.8 2.1 slice-start.1
  221.9 17.0 %copy-start.1 = (bf16[1024,1024]{1,0:T(8,128)(2,1)S(1)}, bf16[1024,1024]{1,0:T(8,128)(2,1)}, u32[]{:S(2)}) copy-start(bf16[1024,1024]{1,0:T(8,128)(2,1)} %param.8) | copy-start | bytes 6291460
Sparse Core Ops, SparseCore 0:
  32.8 140.6 reduce-scatter.1
where the time goes:
time: 246 us
  waiting for transfers between devices  129 us (52%)
  other arithmetic  38.8 us (16%)
  matrix products  23.9 us (10%)
  blocking collectives  23.8 us (10%)
  local copies, waits for them, and re-layouts  16.2 us (7%)
  between operations  14.2 us (6%)
    reduce_scatter x1, waiting for transfers between devices, per_device(): lax.psum_scatter(contract_tokens(hidden, upstream).astype(jnp.bfloat16),...  129 us
    dot_general x1, matrix products, contract_tokens(): lax.dot_general(left, right, (((0,), (0,)), ((), ())), preferred_element_...  23.9 us
    convert_element_type x1, other arithmetic, per_device(): (first_new / (first_peak[:, :, None] + 1e-06)).astype(jnp.bfloat16)  17 us
    unnamed x26, local copies, waits for them, and re-layouts  12.1 us
    pmax x1, blocking collectives, per_device(): row_peak = lax.pmax(row_part, 'col')  12 us
    pmax x1, blocking collectives, per_device(): column_peak = lax.pmax(column_part, ('dp', 'row'))  11.8 us
    reduce_max x1, other arithmetic, per_device(): row_part = jnp.max(second_flat, axis=1)  8.06 us
    unnamed x2, other arithmetic  5.39 us
  transfers between devices with their start and end apart: 1, of which 1 were waited for; matrix products, arithmetic and copies ran while one was open for 5% of the time, Pallas kernels for 0%

commit v1 on v0

v1 whole, which is shorter than its diff:
```python
import functools

import jax
import jax.numpy as jnp
from jax import lax
from jax.experimental import pallas as pl
from jax.experimental.pallas import tpu as pltpu
from jax.sharding import PartitionSpec as P

STEP = 10
CORR_ONE = 1.0 - 0.9**STEP
CORR_TWO = 1.0 - 0.999**STEP
LANES = 128
PARTS = 4
MESH = pl.DeviceIdType.MESH


def contract_tokens(left, right):
    return lax.dot_general(
        left, right, (((0,), (0,)), ((), ())), preferred_element_type=jnp.float32
    )


def update_kernel(
    start, blocks, terms, first, codes_one, scale_ref, codes_two, rows_ref, columns_ref, *refs
):
    term_refs, refs = refs[:terms], refs[terms:]
    if not first:
        row_in, peak_in = refs[3:5]
        refs = refs[5:]
    update_ref, normed_ref, second_ref, row_ref, peak_ref, column_ref = refs
    rows = codes_one.shape[0]
    second_rows = rows_ref[...]
    row_part = None if first else row_in[...]
    if not first:
        peak_ref[...] = peak_in[...]
    for block in range(blocks):
        at = pl.ds(block * LANES, LANES)
        gradient = term_refs[0][:, at].astype(jnp.float32)
        for term in term_refs[1:]:
            gradient += term[:, at].astype(jnp.float32)
        level = codes_one[:, at].astype(jnp.float32)
        upper = level >= 8.0
        expo = jnp.where(upper, level - 8.0, 7.0 - level)
        magnitude = jnp.where(expo > 0.0, jnp.exp2(expo - 7.0), 0.0)
        table = jnp.where(upper, magnitude, -magnitude)
        first_new = (0.9 * scale_ref[:, start + block : start + block + 1]) * table + 0.1 * gradient
        level_two = codes_two[:, at].astype(jnp.float32) * (0.999 / 16.0) + (0.999 / 16.0)
        second_new = (
            jnp.minimum(second_rows, columns_ref[:, at]) * level_two + 0.001 * gradient * gradient
        )
        update_ref[:, at] = (first_new * (1.0 / CORR_ONE)) / (
            jnp.sqrt(second_new * (1.0 / CORR_TWO)) + 1e-08
        )
        peak = jnp.max(jnp.abs(first_new), axis=1, keepdims=True)
        peak_ref[:, start + block : start + block + 1] = peak
        normed_ref[:, at] = (first_new * (1.0 / (peak + 1e-06))).astype(jnp.bfloat16)
        second_ref[:, at] = second_new
        row_part = second_new if row_part is None else jnp.maximum(row_part, second_new)
        column_part = jnp.max(second_new.reshape(rows // 8, 8, LANES), axis=0)

        @pl.when(pl.program_id(0) == 0)
        def _():
            column_ref[:, at] = column_part

        @pl.when(pl.program_id(0) > 0)
        def _():
            column_ref[:, at] = jnp.maximum(column_ref[:, at], column_part)

    row_ref[...] = row_part


def update_part(part, parts, terms, codes_one, scale, codes_two, rows, columns, carried):
    total, width = codes_one.shape
    wide = width // parts
    blocks = wide // LANES
    tall = next(t for t in (256, 224, 192, 128, 112, 64, 32, 16) if total % t == 0)
    here = pl.BlockSpec((tall, wide), lambda i: (i, part))
    specs = [
        here,
        pl.BlockSpec((tall, scale.shape[1]), lambda i: (i, 0)),
        here,
        pl.BlockSpec((tall, 1), lambda i: (i, 0)),
        pl.BlockSpec((1, wide), lambda i: (0, part)),
    ]
    specs += [pl.BlockSpec((tall, wide), lambda i: (i, 0))] * len(terms)
    by_rows = pl.BlockSpec((tall, LANES), lambda i: (i, 0))
    by_blocks = pl.BlockSpec((tall, scale.shape[1]), lambda i: (i, 0))
    operands = [codes_one, scale, codes_two, rows, columns] + terms
    aliases = {}
    if carried is not None:
        aliases = {len(operands) + k: k for k in range(5)}
        operands += list(carried)
        specs += [pl.BlockSpec(memory_space=pl.ANY)] * 3 + [by_rows, by_blocks]
    size = total * wide
    return pl.pallas_call(
        functools.partial(update_kernel, part * blocks, blocks, len(terms), carried is None),
        grid=(total // tall,),
        in_specs=specs,
        out_specs=[
            here,
            here,
            here,
            by_rows,
            by_blocks,
            pl.BlockSpec((8, wide), lambda i: (0, 0)),
        ],
        out_shape=[
            jax.ShapeDtypeStruct((total, width), jnp.float32),
            jax.ShapeDtypeStruct((total, width), jnp.bfloat16),
            jax.ShapeDtypeStruct((total, width), jnp.float32),
            jax.ShapeDtypeStruct((total, LANES), jnp.float32),
            jax.ShapeDtypeStruct(scale.shape, jnp.float32),
            jax.ShapeDtypeStruct((8, wide), jnp.float32),
        ],
        input_output_aliases=aliases,
        compiler_params=pltpu.CompilerParams(vmem_limit_bytes=56 * 2**20),
        cost_estimate=pl.CostEstimate(
            flops=40 * size, bytes_accessed=20 * size, transcendentals=3 * size
        ),
    )(*operands)


def peaks_kernel(
    sizes, row_ref, column_ref, row_out, column_out, row_held, column_held, rs, rr, cs, cr
):
    n_dp, n_row, n_col = sizes
    dp, row, col = lax.axis_index("dp"), lax.axis_index("row"), lax.axis_index("col")
    plane = n_dp * n_row
    me = dp * n_row + row
    along = [{"dp": dp, "row": row, "col": lax.rem(col + d, n_col)} for d in range(1, n_col)]
    across = []
    for d in range(1, plane):
        peer = lax.rem(me + d, plane)
        across.append({"dp": peer // n_row, "row": lax.rem(peer, n_row), "col": col})
    barrier = pltpu.get_barrier_semaphore()
    for peer in along + across:
        pl.semaphore_signal(barrier, inc=1, device_id=peer, device_id_type=MESH)
    pl.semaphore_wait(barrier, len(along) + len(across))
    copies = []
    for source, held, send, recv, peers in (
        (column_ref, column_held, cs, cr, across),
        (row_ref, row_held, rs, rr, along),
    ):
        for slot, peer in enumerate(peers):
            copy = pltpu.make_async_remote_copy(
                src_ref=source,
                dst_ref=held.at[slot],
                send_sem=send.at[slot],
                recv_sem=recv.at[slot],
                device_id=peer,
                device_id_type=MESH,
            )
            copy.start()
            copies.append(copy)
    for copy in copies:
        copy.wait()
    row_out[...] = jnp.maximum(row_ref[...], jnp.max(row_held[...], axis=0))
    column_out[...] = jnp.maximum(column_ref[...], jnp.max(column_held[...], axis=0))


def exchange_peaks(sizes, row_part, column_part):
    def folded(values):
        short = -values.shape[0] % (8 * LANES)
        return jnp.pad(values, (0, short)).reshape(-1, LANES)

    row_fold, column_fold = folded(row_part), folded(column_part)
    n_dp, n_row, n_col = sizes
    others, beside = n_dp * n_row - 1, n_col - 1
    vmem = pl.BlockSpec(memory_space=pltpu.VMEM)
    row_all, column_all = pl.pallas_call(
        functools.partial(peaks_kernel, sizes),
        out_shape=[
            jax.ShapeDtypeStruct(row_fold.shape, jnp.float32),
            jax.ShapeDtypeStruct(column_fold.shape, jnp.float32),
        ],
        in_specs=[vmem, vmem],
        out_specs=[vmem, vmem],
        scratch_shapes=[
            pltpu.VMEM((beside,) + row_fold.shape, jnp.float32),
            pltpu.VMEM((others,) + column_fold.shape, jnp.float32),
            pltpu.SemaphoreType.DMA((beside,)),
            pltpu.SemaphoreType.DMA((beside,)),
            pltpu.SemaphoreType.DMA((others,)),
            pltpu.SemaphoreType.DMA((others,)),
        ],
        compiler_params=pltpu.CompilerParams(collective_id=0, has_side_effects=True),
    )(row_fold, column_fold)
    return (
        row_all.reshape(-1)[: row_part.shape[0]],
        column_all.reshape(-1)[: column_part.shape[0]],
    )


def scatter_terms(n_dp, partial, side):
    bits = n_dp.bit_length() - 1
    if 1 << bits != n_dp:
        return [lax.psum_scatter(partial, "dp", scatter_dimension=0, tiled=True)]
    me = lax.axis_index("dp")
    shape = (2,) * bits + (partial.shape[0] // n_dp, partial.shape[1])
    terms = [partial.reshape(shape)]
    for step in range(bits):
        axis = 0 if side else bits - 1 - step
        bit = bits - 1 - step if side else step
        mine = lax.rem(me // (1 << bit), 2)
        sent = [lax.dynamic_index_in_dim(t, 1 - mine, axis, keepdims=False) for t in terms]
        terms = [lax.dynamic_index_in_dim(t, mine, axis, keepdims=False) for t in terms]
        total = sent[0].astype(jnp.float32)
        for term in sent[1:]:
            total += term.astype(jnp.float32)
        terms.append(
            lax.ppermute(
                total.astype(jnp.bfloat16), "dp", [(i, i ^ (1 << bit)) for i in range(n_dp)]
            )
        )
    return terms


def per_device(
    sizes, hidden, upstream, first_codes, first_scale, second_codes, second_rows, second_columns
):
    columns = first_codes.shape[1]
    wide = columns // PARTS
    both = columns // (PARTS // 2)
    gathered = []
    for pair in range(PARTS // 2):
        partial = contract_tokens(hidden, upstream[:, pair * both : (pair + 1) * both])
        partial = partial.astype(jnp.bfloat16)
        for side in range(2):
            gathered.append(
                scatter_terms(sizes[0], partial[:, side * wide : (side + 1) * wide], side)
            )
    carried, column_parts = None, []
    for part in range(PARTS):
        *carried, column_part = update_part(
            part,
            PARTS,
            gathered[part],
            first_codes,
            first_scale,
            second_codes,
            second_rows[:, None],
            second_columns[None, :],
            carried,
        )
        column_parts.append(column_part)
    update_step, first_normed, second_new, row_part, first_peak = carried
    row_peak, column_peak = exchange_peaks(
        sizes,
        jnp.max(row_part, axis=1),
        jnp.max(jnp.concatenate(column_parts, axis=1), axis=0),
    )
    second_normed = (
        second_new / (jnp.minimum(row_peak[:, None], column_peak[None, :]) + 1e-06)
    ).astype(jnp.bfloat16)
    return update_step, first_normed, first_peak, second_normed, row_peak, column_peak


def solution(mesh):
    placed = (
        P("dp", "row"),
        P("dp", "col"),
        P(("row", "dp"), "col"),
        P(("row", "dp"), "col"),
        P(("row", "dp"), "col"),
        P(("row", "dp")),
        P("col"),
    )
    sizes = (mesh.shape["dp"], mesh.shape["row"], mesh.shape["col"])
    return jax.shard_map(
        functools.partial(per_device, sizes),
        mesh=mesh,
        in_specs=placed,
        out_specs=(
            P(("row", "dp"), "col"),
            P(("row", "dp"), "col"),
            P(("row", "dp"), "col"),
            P(("row", "dp"), "col"),
            P(("row", "dp")),
            P("col"),
        ),
        check_vma=False,
    )
```

time: 246 us -> 190 us (0.77)
  waiting for transfers between devices: 129 us -> 55.1 us
  Pallas kernels: 0 us -> 51 us
  blocking collectives: 23.8 us -> 0 us
  other arithmetic: 38.8 us -> 15.7 us
  local copies, waits for them, and re-layouts: 16.2 us -> 30 us
  between operations: 14.2 us -> 0.81 us
  starting transfers between devices: 0.04 us -> 10.8 us
    reduce_scatter x1 -> x0, waiting for transfers between devices: 129 us -> none  [per_device(): lax.psum_scatter(contract_tokens(hidden, upstream).astype(jnp.bfloat16),...]
    ppermute x0 -> x8, waiting for transfers between devices: none -> 55.1 us  [scatter_terms(): lax.ppermute(total.astype(jnp.bfloat16), 'dp', [(i, i ^ 1 << bit) for i i...]
    pallas_call x0 -> x5, Pallas kernels: none -> 51 us  [the longest x4 42.7 us: update_part(): pl.pallas_call(functools.partial(update_kernel, part * blocks, blocks, le...]
    pmax x2 -> x0, blocking collectives: 23.8 us -> none  [the longest x1 12 us: per_device(): row_peak = lax.pmax(row_part, 'col')]
    squeeze x0 -> x8, local copies, waits for them, and re-layouts: none -> 19.4 us  [the longest x4 11.3 us: scatter_terms(): lax.dynamic_index_in_dim(t, mine, axis, keepdims=False)]
    ppermute x0 -> x8, starting transfers between devices: none -> 10.8 us  [scatter_terms(): lax.ppermute(total.astype(jnp.bfloat16), 'dp', [(i, i ^ 1 << bit) for i i...]
    reduce_max x2, other arithmetic: 11.1 us -> 2.79 us  [the longest x1 1.49 us: per_device(): jnp.max(row_part, axis=1)]
    unnamed x26 -> x23, local copies, waits for them, and re-layouts: 12.1 us -> 4.08 us
  transfers between devices with their start and end apart: 1 -> 8, of which waited for: 1 -> 5; matrix products, arithmetic and copies ran while one was open for 5% -> 22% of each run, Pallas kernels for 0% -> 17%
where the time goes in v1:
time: 190 us; the launch traced here: 188 us
  waiting for transfers between devices  55.1 us (29%)
  Pallas kernels  51 us (27%)
  local copies, waits for them, and re-layouts  30 us (16%)
  matrix products  25.1 us (13%)
  other arithmetic  15.7 us (8%)
  starting transfers between devices  10.8 us (6%)
    ppermute x8, waiting for transfers between devices, scatter_terms(): lax.ppermute(total.astype(jnp.bfloat16), 'dp', [(i, i ^ 1 << bit) for i i...  55.1 us
    pallas_call x4, Pallas kernels, update_part(): pl.pallas_call(functools.partial(update_kernel, part * blocks, blocks, le...  42.7 us
    dot_general x2, matrix products, contract_tokens(): lax.dot_general(left, right, (((0,), (0,)), ((), ())), preferred_element_...  25.1 us
    squeeze x4, local copies, waits for them, and re-layouts, scatter_terms(): lax.dynamic_index_in_dim(t, mine, axis, keepdims=False)  11.3 us
    ppermute x8, starting transfers between devices, scatter_terms(): lax.ppermute(total.astype(jnp.bfloat16), 'dp', [(i, i ^ 1 << bit) for i i...  10.8 us
    pallas_call x1, Pallas kernels, exchange_peaks(): pl.pallas_call(functools.partial(peaks_kernel, sizes), out_shape=[jax.Sha...  8.27 us
    squeeze x4, local copies, waits for them, and re-layouts, scatter_terms(): lax.dynamic_index_in_dim(t, 1 - mine, axis, keepdims=False)  8.17 us
    convert_element_type x4, other arithmetic, scatter_terms(): total.astype(jnp.bfloat16)  7.67 us
  transfers between devices with their start and end apart: 8, of which 5 were waited for; matrix products, arithmetic and copies ran while one was open for 22% of the time, Pallas kernels for 17%

profile of v1, /device:TPU:0, one launch (start us, length us, event | category | flops | bytes accessed | tf_op | source)
XLA Modules:
  0.0 188.5 jit_solution(8789988013196935290)
XLA Ops:
  0.6 11.4 %convolution_convert_fusion = bf16[7168,512]{1,0:T(8,128)(2,1)S(1)} fusion(bf16[1024,7168]{1,0:T(8,128)(2,1)} %param.7, bf16[1024,1024]{1,0:T(8,128)(2,1)} %param.8), kind=kOutput, calls=%fused_computation | convolution fusion | flops 7519862784 | bytes 23068672 | tf_op jit(solution)/shard_map/dot_general | solution.py:19
  12.0 3.5 %fusion.6 = (bf16[7168,256]{1,0:T(8,128)(2,1)}, bf16[7168,256]{1,0:T(8,128)(2,1)}) fusion(bf16[7168,512]{1,0:T(8,128)(2,1)S(1)} %convolution_convert_fusion), kind=kLoop, calls=%fused_computation.28 | loop fusion | bytes 14680064 | tf_op jit(solution)/shard_map/slice | solution.py:231
  15.5 1.6 dynamic-slice_bitcast_fusion
  17.1 3.0 %collective-permute-start.6 = (bf16[2,1792,256]{2,1,0:T(8,128)(2,1)S(1)}, bf16[2,1792,256]{2,1,0:T(8,128)(2,1)}, u32[]{:S(2)}, u32[]{:S(2)}) collective-permute-start(bf16[2,1792,256]{2,1,0:T(8,128)(2,1)S(1)} %dynamic-slice_bitcast_fusion), channel_id=1, source_target_pairs={{0,8},{8,0},{16,24},{24,16},{1,9},{9,1},{17,25},{25,17},{2,10},{10... | collective-permute-start | bytes 5505032 | tf_op jit(solution)/shard_map/ppermute | solution.py:212
  20.1 0.0 copy-start.9
  20.1 3.0 %dynamic-slice_bitcast_fusion.1 = bf16[2,1792,256]{2,1,0:T(8,128)(2,1)} fusion(bf16[2,2,1792,256]{3,2,1,0:T(8,128)(2,1)} %bitcast.64, s32[]{:T(128)S(6)} %select_n.60), kind=kLoop, calls=%fused_computation.12 | loop fusion | bytes 3670020 | tf_op jit(solution)/shard_map/jit(dynamic_index_in_dim)/squeeze | solution.py:206
  23.2 1.5 collective-permute-start.4
  24.7 0.0 copy-done.9
  24.7 13.8 %convolution_convert_fusion.1 = bf16[7168,512]{1,0:T(8,128)(2,1)S(1)} fusion(bf16[1024,7168]{1,0:T(8,128)(2,1)} %param.7, bf16[1024,1024]{1,0:T(8,128)(2,1)S(1)} %copy-done.9), kind=kOutput, calls=%fused_computation.1 | convolution fusion | flops 7519862784 | bytes 23068672 | tf_op jit(solution)/shard_map/dot_general | solution.py:19
  38.5 0.5 fusion.7
  38.9 0.0 copy-start
  38.9 0.0 copy-start.1
  39.0 1.5 dynamic-slice_bitcast_fusion.2
  40.4 0.5 collective-permute-start.2
  41.0 2.0 %dynamic-slice_bitcast_fusion.3 = bf16[2,1792,256]{2,1,0:T(8,128)(2,1)} fusion(bf16[2,2,1792,256]{3,2,1,0:T(8,128)(2,1)S(1)} %bitcast.70, s32[]{:T(128)S(6)} %select_n.60), kind=kLoop, calls=%fused_computation.14 | loop fusion | bytes 3670020 | tf_op jit(solution)/shard_map/jit(dynamic_index_in_dim)/squeeze | solution.py:206
  43.0 0.0 copy-done
  43.0 0.1 copy-done.1
  43.1 0.5 collective-permute-start
  43.6 17.5 %collective-permute-done.6 = bf16[2,1792,256]{2,1,0:T(8,128)(2,1)} collective-permute-done((bf16[2,1792,256]{2,1,0:T(8,128)(2,1)S(1)}, bf16[2,1792,256]{2,1,0:T(8,128)(2,1)}, u32[]{:S(2)}, u32[]{:S(2)}) %collective-permute-start.6) | collective-permute-done | bytes 1835040 | tf_op jit(solution)/shard_map/ppermute | solution.py:212
  61.1 2.6 %fusion = bf16[1792,256]{1,0:T(8,128)(2,1)} fusion(bf16[2,1792,256]{2,1,0:T(8,128)(2,1)} %collective-permute-done.6, s32[]{:T(128)S(6)} %select_n.60, bf16[2,2,1792,256]{3,2,1,0:T(8,128)(2,1)} %bitcast.62, s32[]{:T(128)S(6)} %select_n.63, s32[]{:T(128)S(6)} %select_n.59), kind=kLoop, calls=%fused_computation.4 | loop fusion | flops 1835008 | bytes 2752524 | tf_op jit(solution)/shard_map/convert_element_type | solution.py:213
  63.7 2.1 %collective-permute-start.7 = (bf16[1792,256]{1,0:T(8,128)(2,1)}, bf16[1792,256]{1,0:T(8,128)(2,1)}, u32[]{:S(2)}, u32[]{:S(2)}) collective-permute-start(bf16[1792,256]{1,0:T(8,128)(2,1)} %fusion), channel_id=1, source_target_pairs={{0,16},{8,24},{16,0},{24,8},{1,17},{9,25},{17,1},{25,9},{2,18},{10... | collective-permute-start | bytes 2752520 | tf_op jit(solution)/shard_map/ppermute | solution.py:212
  65.8 0.7 collective-permute-done.4
  66.4 1.7 fusion.1
  68.1 0.9 collective-permute-start.5
  69.0 31.4 %collective-permute-done.2 = bf16[2,1792,256]{2,1,0:T(8,128)(2,1)} collective-permute-done((bf16[2,1792,256]{2,1,0:T(8,128)(2,1)}, bf16[2,1792,256]{2,1,0:T(8,128)(2,1)}, u32[]{:S(2)}, u32[]{:S(2)}) %collective-permute-start.2) | collective-permute-done | bytes 1835040 | tf_op jit(solution)/shard_map/ppermute | solution.py:212
  100.4 1.7 fusion.2
  102.1 0.0 copy-start.2
  102.1 0.0 copy-start.5
  102.1 2.2 %collective-permute-start.3 = (bf16[1792,256]{1,0:T(8,128)(2,1)S(1)}, bf16[1792,256]{1,0:T(8,128)(2,1)}, u32[]{:S(2)}, u32[]{:S(2)}) collective-permute-start(bf16[1792,256]{1,0:T(8,128)(2,1)S(1)} %fusion.2), channel_id=1, source_target_pairs={{0,16},{8,24},{16,0},{24,8},{1,17},{9,25},{17,1},{25,9},{2,18},{10... | collective-permute-start | bytes 2752520 | tf_op jit(solution)/shard_map/ppermute | solution.py:212
  104.3 1.5 collective-permute-done
  105.7 1.7 fusion.3
  107.4 0.1 collective-permute-start.1
  107.5 2.8 %dynamic-slice_bitcast_fusion.5 = (bf16[1792,256]{1,0:T(8,128)(2,1)}, bf16[1792,256]{1,0:T(8,128)(2,1)}) fusion(bf16[2,2,1792,256]{3,2,1,0:T(8,128)(2,1)} %bitcast.63, s32[]{:T(128)S(6)} %select_n.57, s32[]{:T(128)S(6)} %select_n.59, bf16[2,2,1792,256]{3,2,1,0:T(8,128)(2,1)} %bitcast.66), kind=kLoop, calls=%fused_computation.18 | loop fusion | bytes 3670024 | tf_op jit(solution)/shard_map/jit(dynamic_index_in_dim)/squeeze | solution.py:207
  110.4 0.0 copy-done.2
  110.4 1.3 copy.39.scale_ref
  111.6 0.0 copy-done.5
  111.6 1.2 broadcast_in_dim.6.rows_ref
  112.9 2.8 %dynamic-slice_bitcast_fusion.9 = (bf16[1792,256]{1,0:T(8,128)(2,1)}, bf16[1792,256]{1,0:T(8,128)(2,1)}) fusion(bf16[2,2,1792,256]{3,2,1,0:T(8,128)(2,1)} %bitcast.69, s32[]{:T(128)S(6)} %select_n.57, s32[]{:T(128)S(6)} %select_n.59, bf16[2,2,1792,256]{3,2,1,0:T(8,128)(2,1)} %bitcast.72), kind=kLoop, calls=%fused_computation.22 | loop fusion | bytes 3670024 | tf_op jit(solution)/shard_map/jit(dynamic_index_in_dim)/squeeze | solution.py:207
  115.7 2.8 %dynamic-slice_bitcast_fusion.4 = (bf16[1792,256]{1,0:T(8,128)(2,1)}, bf16[1792,256]{1,0:T(8,128)(2,1)}) fusion(bf16[2,1792,256]{2,1,0:T(8,128)(2,1)} %collective-permute-done.6, s32[]{:T(128)S(6)} %select_n.56, bf16[2,1792,256]{2,1,0:T(8,128)(2,1)} %collective-permute-done.2), kind=kLoop, calls=%fused_computation.17 | loop fusion | bytes 3670020 | tf_op jit(solution)/shard_map/jit(dynamic_index_in_dim)/squeeze | solution.py:207
  118.5 2.8 %dynamic-slice_bitcast_fusion.6 = (bf16[1792,256]{1,0:T(8,128)(2,1)}, bf16[1792,256]{1,0:T(8,128)(2,1)}) fusion(bf16[2,1792,256]{2,1,0:T(8,128)(2,1)} %collective-permute-done.4, s32[]{:T(128)S(6)} %select_n.58, bf16[2,1792,256]{2,1,0:T(8,128)(2,1)} %collective-permute-done), kind=kLoop, calls=%fused_computation.19 | loop fusion | bytes 3670020 | tf_op jit(solution)/shard_map/jit(dynamic_index_in_dim)/squeeze | solution.py:207
  121.3 4.1 %collective-permute-done.7.refs_2_ = bf16[1792,256]{1,0:T(8,128)(2,1)} collective-permute-done((bf16[1792,256]{1,0:T(8,128)(2,1)}, bf16[1792,256]{1,0:T(8,128)(2,1)}, u32[]{:S(2)}, u32[]{:S(2)}) %collective-permute-start.7) | collective-permute-done | bytes 917536 | tf_op jit(solution)/shard_map/ppermute | solution.py:212
  125.4 10.3 %shard_map.118 = (f32[1792,1024]{1,0:T(8,128)}, bf16[1792,1024]{1,0:T(8,128)(2,1)}, f32[1792,1024]{1,0:T(8,128)}, f32[1792,128]{1,0:T(8,128)}, f32[1792,8]{1,0:T(8,128)}, /*index=5*/f32[8,256]{1,0:T(8,128)}) custom-call(s32[1792,1024]{1,0:T(8,128)} %codes_one.7, f32[1792,8]{1,0:T(8,128)} %copy.39.scale_ref, s32[1792,1024]{1,0:T(8,128)} %codes_two.7, ...), custom_call_target="tpu_custom_call" | custom-call | flops 18350080 | bytes 9175040 | tf_op jit(solution)/shard_map/pallas_call | solution.py:96
  135.7 0.0 collective-permute-done.5.refs_2_
  135.7 10.8 %shard_map.119 = (f32[1792,1024]{1,0:T(8,128)}, bf16[1792,1024]{1,0:T(8,128)(2,1)}, f32[1792,1024]{1,0:T(8,128)}, f32[1792,128]{1,0:T(8,128)}, f32[1792,8]{1,0:T(8,128)}, /*index=5*/f32[8,256]{1,0:T(8,128)}) custom-call(s32[1792,1024]{1,0:T(8,128)} %codes_one.7, ...), custom_call_target="tpu_custom_call", output_to_operand_aliasing={{0}: (8, {}), {1}: (9, {}), {2}: (10, {}), {3}: (11, {}), {... | custom-call | flops 18350080 | bytes 9175040 | tf_op jit(solution)/shard_map/pallas_call | solution.py:96
  146.5 0.0 collective-permute-done.3.refs_2_
  146.5 10.8 %shard_map.120 = (f32[1792,1024]{1,0:T(8,128)}, bf16[1792,1024]{1,0:T(8,128)(2,1)}, f32[1792,1024]{1,0:T(8,128)}, f32[1792,128]{1,0:T(8,128)}, f32[1792,8]{1,0:T(8,128)}, /*index=5*/f32[8,256]{1,0:T(8,128)}) custom-call(s32[1792,1024]{1,0:T(8,128)} %codes_one.7, ...), custom_call_target="tpu_custom_call", output_to_operand_aliasing={{0}: (8, {}), {1}: (9, {}), {2}: (10, {}), {3}: (11, {}), {... | custom-call | flops 18350080 | bytes 9175040 | tf_op jit(solution)/shard_map/pallas_call | solution.py:96
  157.3 0.0 collective-permute-done.1.refs_2_
  157.3 0.0 copy-start.6
  157.3 0.0 copy-start.7
  157.4 0.0 copy-start.8
  157.4 10.8 %shard_map.121 = (f32[1792,1024]{1,0:T(8,128)}, bf16[1792,1024]{1,0:T(8,128)(2,1)}, f32[1792,1024]{1,0:T(8,128)}, f32[1792,128]{1,0:T(8,128)}, f32[1792,8]{1,0:T(8,128)}, /*index=5*/f32[8,256]{1,0:T(8,128)}) custom-call(s32[1792,1024]{1,0:T(8,128)} %codes_one.7, ...), custom_call_target="tpu_custom_call", output_to_operand_aliasing={{0}: (8, {}), {1}: (9, {}), {2}: (10, {}), {3}: (11, {}), {... | custom-call | flops 18350080 | bytes 9175040 | tf_op jit(solution)/shard_map/pallas_call | solution.py:96
  168.2 1.5 reduce_max.18
  169.7 0.6 pad_bitcast_fusion.row_ref
  170.3 0.0 copy-done.6
  170.3 0.0 copy-done.7
  170.3 0.0 copy-done.8
  170.3 1.3 maximum_reduce_fusion
  171.6 8.3 %shard_map.122 = (f32[16,128]{1,0:T(8,128)}, f32[8,128]{1,0:T(8,128)}) custom-call(f32[16,128]{1,0:T(8,128)} %pad_bitcast_fusion.row_ref, f32[8,128]{1,0:T(8,128)} %bitcast.79), custom_call_target="tpu_custom_call" | custom-call | tf_op jit(solution)/shard_map/pallas_call | solution.py:171
  179.8 0.7 slice_bitcast_fusion
  180.6 2.1 %copy.41 = f32[1792,8]{0,1:T(8,128)} copy(f32[1792,8]{1,0:T(8,128)} %get-tuple-element.66) | data formatting | bytes 114688
  182.6 5.2 %divide_convert_fusion = bf16[1792,1024]{1,0:T(8,128)(2,1)} fusion(f32[1792,1024]{1,0:T(8,128)} %get-tuple-element.50, f32[1024]{0:T(1024)} %bitcast.77, f32[1792]{0:T(1024)S(1)} %slice_bitcast_fusion), kind=kLoop, calls=%fused_computation.2 | loop fusion | flops 7340032 | bytes 11021312 | tf_op jit(solution)/shard_map/convert_element_type | solution.py:255
  187.9 0.0 copy-done.3
  187.9 0.0 copy-done.4
  187.9 0.6 copy.58
  (2 shorter events, 0.0 us)
Async XLA Ops:
  17.1 44.0 %collective-permute-start.6 = (bf16[2,1792,256]{2,1,0:T(8,128)(2,1)S(1)}, bf16[2,1792,256]{2,1,0:T(8,128)(2,1)}, u32[]{:S(2)}, u32[]{:S(2)}) collective-permute-start(bf16[2,1792,256]{2,1,0:T(8,128)(2,1)S(1)} %dynamic-slice_bitcast_fusion), channel_id=1, source_target_pairs={{0,8},{8,0},{16,24},{24,16},{1,9},{9,1},{17,25},{25,17},{2,10},{10... | collective-permute-start | bytes 5505032 | tf_op jit(solution)/shard_map/ppermute | solution.py:212
  20.1 4.6 %copy-start.9 = (bf16[1024,1024]{1,0:T(8,128)(2,1)S(1)}, bf16[1024,1024]{1,0:T(8,128)(2,1)}, u32[]{:S(2)}) copy-start(bf16[1024,1024]{1,0:T(8,128)(2,1)} %param.8) | copy-start | bytes 6291460
  23.2 43.3 %collective-permute-start.4 = (bf16[2,1792,256]{2,1,0:T(8,128)(2,1)}, bf16[2,1792,256]{2,1,0:T(8,128)(2,1)}, u32[]{:S(2)}, u32[]{:S(2)}) collective-permute-start(bf16[2,1792,256]{2,1,0:T(8,128)(2,1)} %dynamic-slice_bitcast_fusion.1), channel_id=1, source_target_pairs={{0,16},{8,24},{16,0},{24,8},{1,17},{9,25},{17,1},{25,9},{2,18},{10... | collective-permute-start | bytes 5505032 | tf_op jit(solution)/shard_map/ppermute | solution.py:212
  38.9 4.1 %copy-start = (bf16[7168,256]{1,0:T(8,128)(2,1)}, bf16[7168,256]{1,0:T(8,128)(2,1)S(1)}, u32[]{:S(2)}) copy-start(bf16[7168,256]{1,0:T(8,128)(2,1)S(1)} %get-tuple-element.72) | copy-start | bytes 11010052
  38.9 4.1 %copy-start.1 = (bf16[7168,256]{1,0:T(8,128)(2,1)}, bf16[7168,256]{1,0:T(8,128)(2,1)S(1)}, u32[]{:S(2)}) copy-start(bf16[7168,256]{1,0:T(8,128)(2,1)S(1)} %get-tuple-element.73) | copy-start | bytes 11010052
  40.4 60.0 %collective-permute-start.2 = (bf16[2,1792,256]{2,1,0:T(8,128)(2,1)}, bf16[2,1792,256]{2,1,0:T(8,128)(2,1)}, u32[]{:S(2)}, u32[]{:S(2)}) collective-permute-start(bf16[2,1792,256]{2,1,0:T(8,128)(2,1)} %dynamic-slice_bitcast_fusion.2), channel_id=1, source_target_pairs={{0,8},{8,0},{16,24},{24,16},{1,9},{9,1},{17,25},{25,17},{2,10},{10... | collective-permute-start | bytes 5505032 | tf_op jit(solution)/shard_map/ppermute | solution.py:212
  43.1 62.7 %collective-permute-start = (bf16[2,1792,256]{2,1,0:T(8,128)(2,1)}, bf16[2,1792,256]{2,1,0:T(8,128)(2,1)}, u32[]{:S(2)}, u32[]{:S(2)}) collective-permute-start(bf16[2,1792,256]{2,1,0:T(8,128)(2,1)} %dynamic-slice_bitcast_fusion.3), channel_id=1, source_target_pairs={{0,16},{8,24},{16,0},{24,8},{1,17},{9,25},{17,1},{25,9},{2,18},{10... | collective-permute-start | bytes 5505032 | tf_op jit(solution)/shard_map/ppermute | solution.py:212
  63.7 61.7 %collective-permute-start.7 = (bf16[1792,256]{1,0:T(8,128)(2,1)}, bf16[1792,256]{1,0:T(8,128)(2,1)}, u32[]{:S(2)}, u32[]{:S(2)}) collective-permute-start(bf16[1792,256]{1,0:T(8,128)(2,1)} %fusion), channel_id=1, source_target_pairs={{0,16},{8,24},{16,0},{24,8},{1,17},{9,25},{17,1},{25,9},{2,18},{10... | collective-permute-start | bytes 2752520 | tf_op jit(solution)/shard_map/ppermute | solution.py:212
  68.1 67.6 %collective-permute-start.5 = (bf16[1792,256]{1,0:T(8,128)(2,1)S(1)}, bf16[1792,256]{1,0:T(8,128)(2,1)}, u32[]{:S(2)}, u32[]{:S(2)}) collective-permute-start(bf16[1792,256]{1,0:T(8,128)(2,1)S(1)} %fusion.1), channel_id=1, source_target_pairs={{0,8},{8,0},{16,24},{24,16},{1,9},{9,1},{17,25},{25,17},{2,10},{10... | collective-permute-start | bytes 2752520 | tf_op jit(solution)/shard_map/ppermute | solution.py:212
  102.1 8.3 %copy-start.2 = (f32[1792,8]{0,1:T(8,128)S(1)}, f32[1792,8]{0,1:T(8,128)}, u32[]{:S(2)}) copy-start(f32[1792,8]{0,1:T(8,128)} %param.10) | copy-start | bytes 172036
  102.1 9.6 %copy-start.5 = (f32[1792]{0:T(1024)S(1)}, f32[1792]{0:T(1024)}, u32[]{:S(2)}) copy-start(f32[1792]{0:T(1024)} %param.12) | copy-start | bytes 21508
  102.1 44.4 %collective-permute-start.3 = (bf16[1792,256]{1,0:T(8,128)(2,1)S(1)}, bf16[1792,256]{1,0:T(8,128)(2,1)}, u32[]{:S(2)}, u32[]{:S(2)}) collective-permute-start(bf16[1792,256]{1,0:T(8,128)(2,1)S(1)} %fusion.2), channel_id=1, source_target_pairs={{0,16},{8,24},{16,0},{24,8},{1,17},{9,25},{17,1},{25,9},{2,18},{10... | collective-permute-start | bytes 2752520 | tf_op jit(solution)/shard_map/ppermute | solution.py:212
  107.4 49.9 %collective-permute-start.1 = (bf16[1792,256]{1,0:T(8,128)(2,1)S(1)}, bf16[1792,256]{1,0:T(8,128)(2,1)}, u32[]{:S(2)}, u32[]{:S(2)}) collective-permute-start(bf16[1792,256]{1,0:T(8,128)(2,1)S(1)} %fusion.3), channel_id=1, source_target_pairs={{0,8},{8,0},{16,24},{24,16},{1,9},{9,1},{17,25},{25,17},{2,10},{10... | collective-permute-start | bytes 2752520 | tf_op jit(solution)/shard_map/ppermute | solution.py:212
  157.3 12.9 %copy-start.6 = (f32[8,256]{1,0:T(8,128)S(1)}, f32[8,256]{1,0:T(8,128)}, u32[]{:S(2)}) copy-start(f32[8,256]{1,0:T(8,128)} %get-tuple-element.52) | copy-start | bytes 24580
  157.3 12.9 %copy-start.7 = (f32[8,256]{1,0:T(8,128)S(1)}, f32[8,256]{1,0:T(8,128)}, u32[]{:S(2)}) copy-start(f32[8,256]{1,0:T(8,128)} %get-tuple-element.53) | copy-start | bytes 24580
  157.4 12.9 %copy-start.8 = (f32[8,256]{1,0:T(8,128)S(1)}, f32[8,256]{1,0:T(8,128)}, u32[]{:S(2)}) copy-start(f32[8,256]{1,0:T(8,128)} %get-tuple-element.54) | copy-start | bytes 24580
  180.5 7.3 %copy-start.3 = (f32[1792]{0:T(1024)}, f32[1792]{0:T(1024)S(1)}, u32[]{:S(2)}) copy-start(f32[1792]{0:T(1024)S(1)} %slice_bitcast_fusion) | copy-start | bytes 21508
  182.6 5.3 %copy-start.4 = (f32[8,128]{1,0:T(8,128)S(1)}, f32[8,128]{1,0:T(8,128)}, u32[]{:S(2)}) copy-start(f32[8,128]{1,0:T(8,128)} %get-tuple-element.57) | copy-start | bytes 12292
